TPU v7x, 512 devices: a whole 4x8x8 slice. The times are simulated.
512 devices in a mesh: row: 16 (over y_hi, x), col: 32 (over y_lo, z, core).
Axes of the slice: x: 4, y: 8 (y_hi: 4, y_lo: 2; y = y_hi * 2 + y_lo), z: 8, core: 2. Of those that a mesh axis runs over, the one named last changes fastest.
Arguments:
- tokens: bfloat16 [256, 12288], P('col', 'row'), may hold values from -6 to 6
- cotangent: bfloat16 [256, 12288], P('col', 'row'), may hold values from -3 to 3
- weight_in: bfloat16 [12288, 24576], P('row', 'col'), may hold values from -0.0546875 to 0.0546875
- weight_out: bfloat16 [24576, 12288], P('col', 'row'), may hold values from -0.0390625 to 0.0390625
Outputs:
- mixed: bfloat16 [256, 12288], P('col', 'row')
- grad_tokens: bfloat16 [256, 12288], P('col', 'row')
- grad_in: bfloat16 [12288, 24576], P('row', 'col')
- grad_out: bfloat16 [24576, 12288], P('col', 'row')
All inputs are finite; a program needn't handle non-finite values.
Results may differ from a plain program's by a relative error of at most 0.0049.
Values may be sent and summed in bfloat16 or wider, within the bound.
A program may use at most 64 MiB of HBM per device.

v0:
```python
import jax
import jax.numpy as jnp
from jax import lax
from jax.sharding import PartitionSpec as P


def gelu_parts(pre_act):
    normal_cdf = 0.5 * (1.0 + jax.scipy.special.erf(pre_act * 0.7071067811865476))
    density = jnp.exp(-0.5 * pre_act * pre_act) * 0.3989422804014327
    return (pre_act * normal_cdf, normal_cdf + pre_act * density)


def contract_first(left_side, right_side):
    return lax.dot_general(
        left_side, right_side, (((0,), (0,)), ((), ())), preferred_element_type=jnp.float32
    )


def contract_last(left_side, right_side):
    return lax.dot_general(
        left_side, right_side, (((1,), (1,)), ((), ())), preferred_element_type=jnp.float32
    )


def width_sums(term_fn, row_count):
    return lax.psum_scatter(
        term_fn(jnp.int32(0), lax.axis_size("row") * row_count),
        "row",
        scatter_dimension=0,
        tiled=True,
    )


def token_spread(row_piece):
    return lax.all_gather(row_piece, "row", axis=0, tiled=True)


def unit_sums(term_fn, row_count):
    return lax.psum_scatter(
        term_fn(jnp.int32(0), lax.axis_size("col") * row_count),
        "col",
        scatter_dimension=0,
        tiled=True,
    )


def shards(tokens, cotangent, weight_in, weight_out):
    tok_all, cot_all = (
        lax.all_gather(tokens, "col", axis=0, tiled=True),
        lax.all_gather(cotangent, "col", axis=0, tiled=True),
    )
    total_rows = tok_all.shape[0]
    share_rows = total_rows // lax.axis_size("row")
    col_rows = total_rows // lax.axis_size("col")

    def forward_term(first_row, row_count):
        return jnp.dot(tok_all, weight_in, preferred_element_type=jnp.float32)

    def backward_term(first_row, row_count):
        return contract_last(cot_all, weight_out)

    pre_share = width_sums(forward_term, share_rows)
    gelu_value, gelu_slope = gelu_parts(pre_share)
    hidden = token_spread(gelu_value.astype(jnp.bfloat16))
    grad_share = width_sums(backward_term, share_rows)
    grad_pre = token_spread((grad_share * gelu_slope).astype(jnp.bfloat16))

    def mix_term(first_row, row_count):
        return jnp.dot(hidden, weight_out, preferred_element_type=jnp.float32)

    def input_term(first_row, row_count):
        return contract_last(grad_pre, weight_in)

    mixed = unit_sums(mix_term, col_rows).astype(jnp.bfloat16)
    grad_in = contract_first(tok_all, grad_pre).astype(jnp.bfloat16)
    grad_out = contract_first(hidden, cot_all).astype(jnp.bfloat16)
    grad_tokens = unit_sums(input_term, col_rows).astype(jnp.bfloat16)
    return (mixed, grad_tokens, grad_in, grad_out)


def solution(mesh):
    return jax.shard_map(
        shards,
        mesh=mesh,
        in_specs=(P("col", "row"), P("col", "row"), P("row", "col"), P("col", "row")),
        out_specs=(P("col", "row"), P("col", "row"), P("row", "col"), P("col", "row")),
        check_vma=False,
    )
```

profile of v0, /device:TPU:4, one launch (start us, length us, event | category | flops | bytes accessed | tf_op | source)
XLA Modules:
  0.0 521.1 jit_solution(5491140594892650039)
XLA Ops:
  7.2 0.0 reduce-scatter.9.cloned.1.call-start
  7.2 41.8 %all_gather.14 = bf16[256,768]{1,0:T(8,128)(2,1)S(1)} all-gather(bf16[8,768]{1,0:T(8,128)(2,1)} %param.5), channel_id=1, replica_groups=mesh['row'=16,'col'=32] {'col'}, dimensions={0}, use_global_device_ids=true | all-gather | bytes 405504 | tf_op jit(solution)/shard_map/all_gather | solution.py:50
  49.1 1.4 fusion.9
  50.5 0.0 reduce-scatter.9.cloned.1.call-update
  50.5 0.0 reduce-scatter.5.cloned.1.call-start
  50.5 32.1 %all_gather.12 = bf16[256,768]{1,0:T(8,128)(2,1)S(1)} all-gather(bf16[8,768]{1,0:T(8,128)(2,1)S(1)} %copy-done.3), channel_id=1, replica_groups=mesh['row'=16,'col'=32] {'col'}, dimensions={0}, use_global_device_ids=true | all-gather | bytes 405504 | tf_op jit(solution)/shard_map/all_gather | solution.py:49
  82.6 1.4 fusion.7
  84.0 0.0 reduce-scatter.7.cloned.1.call-start
  84.0 52.5 %reduce-scatter.9.cloned.1.call-done = f32[16,768]{1,0:T(8,128)} async-done(((f32[256,768]{1,0:T(8,128)}), f32[16,768]{1,0:T(8,128)}) %reduce-scatter.9.cloned.1.call-update) | async-done | bytes 49168 | tf_op jit(solution)/shard_map/reduce_scatter | solution.py:26
  136.5 94.0 %reduce-scatter.5.cloned.1.call-done = f32[16,768]{1,0:T(8,128)} async-done(((f32[256,768]{1,0:T(8,128)}), f32[16,768]{1,0:T(8,128)}) %reduce-scatter.5.cloned.1.call-update) | async-done | bytes 49168 | tf_op jit(solution)/shard_map/reduce_scatter | solution.py:26
  230.5 1.5 fusion.6
  232.0 40.0 %all_gather.13 = bf16[256,768]{1,0:T(8,128)(2,1)S(1)} all-gather(bf16[16,768]{1,0:T(8,128)(2,1)S(1)} %get-tuple-element.9), channel_id=1, replica_groups=mesh['row'=16,'col'=32] {'row'}, dimensions={0}, use_global_device_ids=true | all-gather | bytes 417792 | tf_op jit(solution)/shard_map/all_gather | solution.py:35
  272.0 1.4 fusion.8
  273.4 0.0 reduce-scatter.11.cloned.1.call-start
  273.4 40.7 %all_gather.15 = bf16[256,768]{1,0:T(8,128)(2,1)S(1)} all-gather(bf16[16,768]{1,0:T(8,128)(2,1)} %get-tuple-element.8), channel_id=1, replica_groups=mesh['row'=16,'col'=32] {'row'}, dimensions={0}, use_global_device_ids=true | all-gather | bytes 417792 | tf_op jit(solution)/shard_map/all_gather | solution.py:35
  314.2 0.7 copy-done.2
  314.9 1.4 fusion.10
  316.3 1.5 fusion
  317.8 1.5 copy.8
  319.3 1.5 convolution_convert_fusion
  320.8 74.8 %reduce-scatter.7.cloned.1.call-done = f32[8,768]{1,0:T(8,128)} async-done(((f32[256,768]{1,0:T(8,128)}), f32[8,768]{1,0:T(8,128)}) %reduce-scatter.7.cloned.1.call-update) | async-done | bytes 24592 | tf_op jit(solution)/shard_map/reduce_scatter | solution.py:39
  395.7 1.3 convert_element_type.22
  397.0 116.2 %reduce-scatter.11.cloned.1.call-done = f32[8,768]{1,0:T(8,128)} async-done(((f32[256,768]{1,0:T(8,128)}), f32[8,768]{1,0:T(8,128)}) %reduce-scatter.11.cloned.1.call-update) | async-done | bytes 24592 | tf_op jit(solution)/shard_map/reduce_scatter | solution.py:39
  513.2 1.3 convert_element_type.24
  (10 shorter events, 0.1 us)
Async XLA Ops:
  7.2 41.9 %copy-start = (bf16[768,768]{1,0:T(8,128)(2,1)S(1)}, bf16[768,768]{1,0:T(8,128)(2,1)}, u32[]{:S(2)}) copy-start(bf16[768,768]{1,0:T(8,128)(2,1)} %param.7) | copy-start | bytes 3538948
  7.2 129.3 %reduce-scatter.9.cloned.1.call-start = ((), (), s32[]{:S(2)}) async-start(), calls=%async_computation.6 | async-start | bytes 835584 | tf_op jit(solution)/shard_map/reduce_scatter | solution.py:26
  49.1 1.5 copy-start.3
  50.5 32.1 %copy-start.1 = (bf16[768,768]{1,0:T(8,128)(2,1)S(1)}, bf16[768,768]{1,0:T(8,128)(2,1)}, u32[]{:S(2)}) copy-start(bf16[768,768]{1,0:T(8,128)(2,1)} %param.6) | copy-start | bytes 3538948
  50.5 180.0 %reduce-scatter.5.cloned.1.call-start = ((), (), s32[]{:S(2)}) async-start(), calls=%async_computation.4 | async-start | bytes 835584 | tf_op jit(solution)/shard_map/reduce_scatter | solution.py:26
  84.0 311.7 %reduce-scatter.7.cloned.1.call-start = ((), (), s32[]{:S(2)}) async-start(), calls=%async_computation.5 | async-start | bytes 811008 | tf_op jit(solution)/shard_map/reduce_scatter | solution.py:39
  273.4 239.8 %reduce-scatter.11.cloned.1.call-start = ((), (), s32[]{:S(2)}) async-start(), calls=%async_computation.7 | async-start | bytes 811008 | tf_op jit(solution)/shard_map/reduce_scatter | solution.py:39
  314.2 0.7 copy-start.2
Sparse Core Ops, SparseCore 0:
  50.6 85.8 reduce-scatter.8
  141.1 89.3 reduce-scatter.4
  273.5 122.1 reduce-scatter.6
  398.5 114.6 reduce-scatter.10
where the time goes:
time: 521 us
  waiting for transfers between devices  338 us (65%)
  blocking collectives  155 us (30%)
  between operations  13.8 us (3%)
  matrix products  8.55 us (2%)
    reduce_scatter x2, waiting for transfers between devices, unit_sums(): lax.psum_scatter(term_fn(jnp.int32(0), lax.axis_size('col') * row_count),...  191 us
    reduce_scatter x2, waiting for transfers between devices, width_sums(): lax.psum_scatter(term_fn(jnp.int32(0), lax.axis_size('row') * row_count),...  146 us
    all_gather x2, blocking collectives, token_spread(): return lax.all_gather(row_piece, 'row', axis=0, tiled=True)  80.7 us
    all_gather x1, blocking collectives, shards(): lax.all_gather(cotangent, 'col', axis=0, tiled=True)  41.8 us
    all_gather x1, blocking collectives, shards(): lax.all_gather(tokens, 'col', axis=0, tiled=True)  32.1 us
  transfers between devices with their start and end apart: 4, of which 4 were waited for; matrix products, arithmetic and copies ran while one was open for 2% of the time, Pallas kernels for 0%

commit v1 on v0

v1 whole, which is shorter than its diff:
```python
import jax
import jax.numpy as jnp
from jax import lax
from jax.experimental import pallas as pl
from jax.experimental.pallas import tpu as pltpu
from jax.sharding import PartitionSpec as P

MESH = pl.DeviceIdType.MESH
BF16, F32 = jnp.bfloat16, jnp.float32
NX, NY, NP, NZ, NK = 4, 4, 2, 8, 2
Z_ORDER = (2, 6, 1, 5, 3, 7, 4)


def gelu_parts(pre_act):
    normal_cdf = 0.5 * (1.0 + jax.scipy.special.erf(pre_act * 0.7071067811865476))
    density = jnp.exp(-0.5 * pre_act * pre_act) * 0.3989422804014327
    return pre_act * normal_cdf, normal_cdf + pre_act * density


def dot(left, right, dims):
    return lax.dot_general(left, right, (dims, ((), ())), preferred_element_type=F32)


def kernel(
    tok_ref, cot_ref, wi_hbm, wo_hbm,
    mixed_ref, gt_ref, gi_hbm, go_hbm,
    wi, wo, gat, tok, cot, own, xs, xr, ys, yr, act,
    part, ss, sr, ps, pr, zs, zr, gi, go,
    w_sem, g_sem,
    az_s, az_r, ay_s, ay_r, ak_s, ak_r,
    rx_s, rx_r, ry_s, ry_r,
    cy_s, cy_r, cx_s, cx_r,
    dk_s, dk_r, dy_s, dy_r, dz_s, dz_r,
):
    r, c = lax.axis_index("row"), lax.axis_index("col")
    yh, x = r // NX, lax.rem(r, NX)
    p, z, k = c // (NZ * NK), lax.rem(c // NK, NZ), lax.rem(c, NK)
    nk, np_ = 1 - k, 1 - p

    def col_dev(p_, z_, k_):
        return (r, p_ * (NZ * NK) + z_ * NK + k_)

    def row_dev(yh_, x_):
        return (yh_ * NX + x_, c)

    def add(a, d, n):
        return lax.rem(a + d + n, n)

    x_dev = [row_dev(yh, add(x, d, NX)) for d in range(NX)]
    y_dev = [row_dev(add(yh, d, NY), x) for d in range(NY)]
    z_dev = [col_dev(p, add(z, d, NZ), k) for d in range(NZ)]
    p_dev, k_dev = col_dev(np_, z, k), col_dev(p, z, nk)

    def copy(src, dst, s_sem, r_sem, device):
        return pltpu.make_async_remote_copy(
            src_ref=src, dst_ref=dst, send_sem=s_sem, recv_sem=r_sem,
            device_id=device, device_id_type=MESH,
        )

    load_wi = pltpu.make_async_copy(wi_hbm, wi, w_sem.at[0])
    load_wo = pltpu.make_async_copy(wo_hbm, wo, w_sem.at[1])
    load_wi.start()
    load_wo.start()

    peers = x_dev[1:] + y_dev[1:] + z_dev[1:] + [p_dev, k_dev]
    barrier = pltpu.get_barrier_semaphore()
    for peer in peers:
        pl.semaphore_signal(barrier, inc=1, device_id=peer, device_id_type=MESH)
    q_me = p * NZ + z
    gat[k, q_me] = jnp.concatenate(
        [tok_ref[...].astype(F32), cot_ref[...].astype(F32)], axis=0
    ).astype(BF16)
    pl.semaphore_wait(barrier, len(peers))

    sends = []

    def start(*args):
        one = copy(*args)
        one.start()
        sends.append(one)

    def gat_at(k_, p_, d):
        return gat.at[k_, p_ * NZ + add(z, -d, NZ)]

    def z_copy(d):
        return copy(gat.at[k, q_me], gat.at[k, q_me], az_s.at[d], az_r.at[d], z_dev[d])

    def z_arrived(d):
        blk = gat_at(k, p, d)
        copy(blk, blk, az_s.at[d], az_r.at[d], z_dev[d]).wait_recv()

    def forward(d):
        blk = gat_at(k, p, d)
        start(blk, blk, ay_s.at[d], ay_r.at[d], p_dev)
        start(blk, blk, ak_s.at[0, d], ak_r.at[0, d], k_dev)

    def forward_pair(d):
        blk = gat_at(k, np_, d)
        copy(blk, blk, ay_s.at[d], ay_r.at[d], p_dev).wait_recv()
        start(blk, blk, ak_s.at[1, d], ak_r.at[1, d], k_dev)

    def core_arrived(d):
        for side, p_ in ((0, p), (1, np_)):
            blk = gat_at(nk, p_, d)
            copy(blk, blk, ak_s.at[side, d], ak_r.at[side, d], k_dev).wait_recv()

    for d in Z_ORDER:
        one = z_copy(d)
        one.start()
        sends.append(one)
    forward(0)

    def row_terms(d0):
        core_arrived(d0)
        core_arrived(d0 + 4)
        xt = lax.rem(z - d0 + NZ, NX)
        for j in range(NY):
            q = j * NX + xt
            one, two = gat[0, q].astype(F32), gat[1, q].astype(F32)
            tok[xt, pl.ds(16 * j, 16), :] = jnp.concatenate([one[:8], two[:8]], 0).astype(BF16)
            cot[xt, pl.ds(16 * j, 16), :] = jnp.concatenate([one[8:], two[8:]], 0).astype(BF16)
        dx = lax.rem(xt - x + NX, NX)
        for s in range(2):
            if s == 0:
                term = dot(tok[xt], wi[...], ((1,), (0,)))
            else:
                term = dot(cot[xt], wo[...], ((1,), (1,)))

            @pl.when(dx == 0)
            def _():
                own[s] = term.reshape(NY, 16, 768)

            @pl.when(dx != 0)
            def _():
                xs[xt, s] = term.astype(BF16).reshape(NY, 16, 768)
                copy(
                    xs.at[xt, s], xr.at[dx, s], rx_s.at[dx, s], rx_r.at[dx, s],
                    row_dev(yh, xt),
                ).start()

    z_arrived(2)
    forward(2)
    z_arrived(6)
    forward(6)
    forward_pair(0)
    z_arrived(1)
    forward(1)
    forward_pair(2)
    z_arrived(5)
    forward(5)
    forward_pair(6)
    load_wi.wait()
    load_wo.wait()
    row_terms(2)
    forward_pair(1)
    z_arrived(3)
    forward(3)
    forward_pair(5)
    z_arrived(7)
    forward(7)
    row_terms(1)
    forward_pair(3)
    z_arrived(4)
    forward(4)
    forward_pair(7)
    forward_pair(4)
    row_terms(3)
    row_terms(0)

    for d in range(1, NX):
        for s in range(2):
            one = copy(xs.at[0, s], xr.at[d, s], rx_s.at[d, s], rx_r.at[d, s], x_dev[d])
            one.wait_recv()
            one.wait_send()

    def x_sum(j, s):
        return (
            own[s, j] + xr[1, s, j].astype(F32) + xr[2, s, j].astype(F32) + xr[3, s, j].astype(F32)
        )

    for d in (2, 1, 3):
        j = add(yh, d, NY)
        for s in range(2):
            ys[d, s] = x_sum(j, s).astype(BF16)
        start(ys.at[d], yr.at[d], ry_s.at[d], ry_r.at[d], y_dev[d])
    sums = [x_sum(yh, s) for s in range(2)]
    for d in (1, 3, 2):
        copy(ys.at[d], yr.at[d], ry_s.at[d], ry_r.at[d], y_dev[d]).wait_recv()
        sums = [sums[s] + yr[d, s].astype(F32) for s in range(2)]
    value, slope = gelu_parts(sums[0])
    act[x, yh, 0] = value.astype(BF16)
    act[x, yh, 1] = (sums[1] * slope).astype(BF16)

    mine = act.at[x, yh]
    for d in (2, 1, 3):
        start(mine, mine, cy_s.at[d], cy_r.at[d], y_dev[d])
    for d in (0, 1, 3, 2):
        blk = act.at[x, add(yh, -d, NY)]
        if d:
            copy(blk, blk, cy_s.at[d], cy_r.at[d], y_dev[d]).wait_recv()
        for e in (2, 1, 3):
            start(blk, blk, cx_s.at[d, e], cx_r.at[d, e], x_dev[e])

    for e in (0, 1, 3, 2):
        xt = add(x, -e, NX)
        if e:
            for d in (0, 1, 3, 2):
                blk = act.at[xt, add(yh, -d, NY)]
                copy(blk, blk, cx_s.at[d, e], cx_r.at[d, e], x_dev[e]).wait_recv()
        mix = dot(act[xt, :, 0].reshape(64, 768), wo[...], ((1,), (0,)))
        gtk = dot(act[xt, :, 1].reshape(64, 768), wi[...], ((1,), (1,)))
        for j in range(NY):
            two = [
                jnp.concatenate([mix[16 * j + 8 * i:16 * j + 8 * i + 8], gtk[16 * j + 8 * i:16 * j + 8 * i + 8]], 0)
                for i in range(2)
            ]
            part[e, j] = jnp.where(k == 0, two[0], two[1])
            ss[e, j] = jnp.where(k == 0, two[1], two[0])
        start(ss.at[e], sr.at[e], dk_s.at[e], dk_r.at[e], k_dev)

    def grad(left, right, out, hbm, sem):
        for m in range(3):
            cols = pl.ds(256 * m, 256)
            out[:, cols] = dot(left, right[:, 256 * m:256 * m + 256], ((0,), (0,))).astype(BF16)
        pltpu.make_async_copy(out, hbm, sem).start()

    for e in (0, 1, 3, 2):
        copy(ss.at[e], sr.at[e], dk_s.at[e], dk_r.at[e], k_dev).wait_recv()
        for i in range(2):
            j = 2 * np_ + i
            ps[e, i] = (part[e, j] + sr[e, j]).astype(BF16)
        start(ps.at[e], pr.at[e], dy_s.at[e], dy_r.at[e], p_dev)

    grad(tok[...].reshape(256, 768), act[:, :, 1].reshape(256, 768), gi, gi_hbm, g_sem.at[0])

    for e in (0, 1, 3, 2):
        copy(ps.at[e], pr.at[e], dy_s.at[e], dy_r.at[e], p_dev).wait_recv()
        for i in range(2):
            j = 2 * p + i
            zt = NX * i + add(x, -e, NX)
            total = part[e, j] + sr[e, j] + pr[e, i].astype(F32)
            dz = lax.rem(zt - z + NZ, NZ)

            @pl.when(dz == 0)
            def _():
                part[0, 2 * np_] = total

            @pl.when(dz != 0)
            def _():
                zs[dz] = total.astype(BF16)
                copy(
                    zs.at[dz], zr.at[dz], dz_s.at[dz], dz_r.at[dz], col_dev(p, zt, k)
                ).start()

    grad(act[:, :, 0].reshape(256, 768), cot[...].reshape(256, 768), go, go_hbm, g_sem.at[1])

    total = part[0, 2 * np_]
    for d in range(1, NZ):
        one = copy(zs.at[d], zr.at[d], dz_s.at[d], dz_r.at[d], z_dev[d])
        one.wait_recv()
        one.wait_send()
        total = total + zr[d].astype(F32)
    mixed_ref[...] = total[:8].astype(BF16)
    gt_ref[...] = total[8:].astype(BF16)

    for one in sends:
        one.wait_send()
    pltpu.make_async_copy(gi, gi_hbm, g_sem.at[0]).wait()
    pltpu.make_async_copy(go, go_hbm, g_sem.at[1]).wait()


def shards(tokens, cotangent, weight_in, weight_out):
    dma = pltpu.SemaphoreType.DMA
    vmem, hbm = pl.BlockSpec(memory_space=pltpu.VMEM), pl.BlockSpec(memory_space=pl.ANY)
    shape = lambda a: jax.ShapeDtypeStruct(a.shape, BF16)
    sem = lambda *n: [dma(n), dma(n)]
    return pl.pallas_call(
        kernel,
        out_shape=(shape(tokens), shape(tokens), shape(weight_in), shape(weight_out)),
        in_specs=[vmem, vmem, hbm, hbm],
        out_specs=(vmem, vmem, hbm, hbm),
        scratch_shapes=[
            pltpu.VMEM((768, 768), BF16),
            pltpu.VMEM((768, 768), BF16),
            pltpu.VMEM((NK, NP * NZ, 16, 768), BF16),
            pltpu.VMEM((NX, 64, 768), BF16),
            pltpu.VMEM((NX, 64, 768), BF16),
            pltpu.VMEM((2, NY, 16, 768), F32),
            pltpu.VMEM((NX, 2, NY, 16, 768), BF16),
            pltpu.VMEM((NX, 2, NY, 16, 768), BF16),
            pltpu.VMEM((NY, 2, 16, 768), BF16),
            pltpu.VMEM((NY, 2, 16, 768), BF16),
            pltpu.VMEM((NX, NY, 2, 16, 768), BF16),
            pltpu.VMEM((NX, NY, 16, 768), F32),
            pltpu.VMEM((NX, NY, 16, 768), F32),
            pltpu.VMEM((NX, NY, 16, 768), F32),
            pltpu.VMEM((NX, 2, 16, 768), BF16),
            pltpu.VMEM((NX, 2, 16, 768), BF16),
            pltpu.VMEM((NZ, 16, 768), BF16),
            pltpu.VMEM((NZ, 16, 768), BF16),
            pltpu.VMEM((768, 768), BF16),
            pltpu.VMEM((768, 768), BF16),
            dma((2,)),
            dma((2,)),
            *sem(NZ), *sem(NZ), *sem(2, NZ),
            *sem(NX, 2), *sem(NY),
            *sem(NY), *sem(NY, NX),
            *sem(NX), *sem(NX), *sem(NZ),
        ],
        compiler_params=pltpu.CompilerParams(
            collective_id=0, has_side_effects=True, vmem_limit_bytes=48 * 2**20
        ),
    )(tokens, cotangent, weight_in, weight_out)


def solution(mesh):
    return jax.shard_map(
        shards,
        mesh=mesh,
        in_specs=(P("col", "row"), P("col", "row"), P("row", "col"), P("col", "row")),
        out_specs=(P("col", "row"), P("col", "row"), P("row", "col"), P("col", "row")),
        check_vma=False,
    )
```

time: 521 us -> 83.1 us (0.16)
  the two profiles are of different devices: /device:TPU:4 before, /device:TPU:10 now
where the time goes in v1:
time: 83.1 us; the launch traced here: 82.8 us
  Pallas kernels  74.9 us (90%)
  local copies, waits for them, and re-layouts  7.17 us (9%)
    pallas_call x1, Pallas kernels, shards(): pl.pallas_call(kernel, out_shape=(shape(tokens), shape(tokens), shape(wei...  74.9 us
    unnamed x12, local copies, waits for them, and re-layouts  7.17 us

profile of v1, /device:TPU:10, one launch (start us, length us, event | category | flops | bytes accessed | tf_op | source)
XLA Modules:
  0.0 82.8 jit_solution(38174263135665080)
XLA Ops:
  0.6 0.0 copy-start
  0.6 1.3 %copy-done = bf16[768,768]{1,0:T(8,128)(2,1)S(1)} copy-done((bf16[768,768]{1,0:T(8,128)(2,1)S(1)}, bf16[768,768]{1,0:T(8,128)(2,1)}, u32[]{:S(2)}) %copy-start) | copy-done | bytes 1179672
  1.9 0.0 copy-start.1
  1.9 1.3 %copy-done.1 = bf16[768,768]{1,0:T(8,128)(2,1)S(1)} copy-done((bf16[768,768]{1,0:T(8,128)(2,1)S(1)}, bf16[768,768]{1,0:T(8,128)(2,1)}, u32[]{:S(2)}) %copy-start.1) | copy-done | bytes 1179672
  3.2 0.0 copy-start.2
  3.2 0.7 copy-done.2
  3.9 0.0 copy-start.3
  3.9 0.7 copy-done.3
  4.6 74.9 %shard_map.75 = (bf16[8,768]{1,0:T(8,128)(2,1)S(1)}, bf16[8,768]{1,0:T(8,128)(2,1)S(1)}, bf16[768,768]{1,0:T(8,128)(2,1)S(1)}, bf16[768,768]{1,0:T(8,128)(2,1)S(1)}) custom-call(bf16[8,768]{1,0:T(8,128)(2,1)S(1)} %copy-done.2, bf16[8,768]{1,0:T(8,128)(2,1)S(1)} %copy-done.3, bf16[768,768]{1,0:T(8,128)(2,1)S(1)} %copy-done, bf16[768,768]{1,0:T(8,128)(2,1)S(1)} %copy-done.1), custom_call_target="tpu_custom_call" | custom-call | tf_op jit(solution)/shard_map/pallas_call | solution.py:277
  79.5 0.6 copy.12
  80.1 0.6 copy.13
  80.7 1.0 %copy.14 = bf16[768,768]{1,0:T(8,128)(2,1)} copy(bf16[768,768]{1,0:T(8,128)(2,1)S(1)} %get-tuple-element.10) | data formatting | bytes 2359296
  81.8 1.0 %copy.15 = bf16[768,768]{1,0:T(8,128)(2,1)} copy(bf16[768,768]{1,0:T(8,128)(2,1)S(1)} %get-tuple-element.11) | data formatting | bytes 2359296
Async XLA Ops:
  0.6 1.3 %copy-start = (bf16[768,768]{1,0:T(8,128)(2,1)S(1)}, bf16[768,768]{1,0:T(8,128)(2,1)}, u32[]{:S(2)}) copy-start(bf16[768,768]{1,0:T(8,128)(2,1)} %wi_hbm.1) | copy-start | bytes 3538948
  1.9 1.3 %copy-start.1 = (bf16[768,768]{1,0:T(8,128)(2,1)S(1)}, bf16[768,768]{1,0:T(8,128)(2,1)}, u32[]{:S(2)}) copy-start(bf16[768,768]{1,0:T(8,128)(2,1)} %wo_hbm.1) | copy-start | bytes 3538948
  3.2 0.7 copy-start.2
  3.9 0.7 copy-start.3

commit v2 on v0

v2 whole, which is shorter than its diff:
```python
import jax
import jax.numpy as jnp
from jax import lax
from jax.experimental import pallas as pl
from jax.experimental.pallas import tpu as pltpu
from jax.sharding import PartitionSpec as P

MESH = pl.DeviceIdType.MESH
BF16, F32 = jnp.bfloat16, jnp.float32
NX, NY, NP, NZ, NK = 4, 4, 2, 8, 2
NS = 2
WIDTH, HALF = 768, 384
Z_ORDER = (4, 3, 5, 1, 7, 2, 6)


def gelu_parts(pre_act):
    normal_cdf = 0.5 * (1.0 + jax.scipy.special.erf(pre_act * 0.7071067811865476))
    density = jnp.exp(-0.5 * pre_act * pre_act) * 0.3989422804014327
    return pre_act * normal_cdf, normal_cdf + pre_act * density


def dot(left, right, dims):
    return lax.dot_general(left, right, (dims, ((), ())), preferred_element_type=F32)


def fold(rows):
    return jnp.concatenate([rows[:, :HALF], rows[:, HALF:]], axis=0)


def unfold(block):
    return jnp.concatenate([block[:8], block[8:]], axis=1)


def kernel(
    tok_hbm, cot_hbm, wi_hbm, wo_hbm,
    mixed_ref, gt_ref, gi, go,
    weights, first, gat, rows, own, xs, xr, ys, yr, slopes, act,
    part, ss, sr, ps, pr, zs, zr,
    w_sem,
    az_s, az_r, ay_s, ay_r, ak_s, ak_r,
    rx_s, rx_r, ry_s, ry_r,
    cy_s, cy_r, cx_s, cx_r,
    dk_s, dk_r, dy_s, dy_r, dz_s, dz_r,
):
    r, c = lax.axis_index("row"), lax.axis_index("col")
    yh, x = r // NX, lax.rem(r, NX)
    p, z, k = c // (NZ * NK), lax.rem(c // NK, NZ), lax.rem(c, NK)
    nk, np_ = 1 - k, 1 - p

    def col_dev(p_, z_, k_):
        return (r, p_ * (NZ * NK) + z_ * NK + k_)

    def row_dev(yh_, x_):
        return (yh_ * NX + x_, c)

    def add(a, d, n):
        return lax.rem(a + d + n, n)

    x_dev = [row_dev(yh, add(x, d, NX)) for d in range(NX)]
    y_dev = [row_dev(add(yh, d, NY), x) for d in range(NY)]
    z_dev = [col_dev(p, add(z, d, NZ), k) for d in range(NZ)]
    p_dev, k_dev = col_dev(np_, z, k), col_dev(p, z, nk)

    def copy(src, dst, s_sem, r_sem, device):
        return pltpu.make_async_remote_copy(
            src_ref=src, dst_ref=dst, send_sem=s_sem, recv_sem=r_sem,
            device_id=device, device_id_type=MESH,
        )

    sends = []

    def start(*args):
        one = copy(*args)
        one.start()
        sends.append(one)

    loads = [
        pltpu.make_async_copy(src, dst, w_sem.at[n])
        for n, (src, dst) in enumerate(
            ((tok_hbm, first.at[0]), (cot_hbm, first.at[1]), (wi_hbm, weights.at[0]), (wo_hbm, weights.at[1]))
        )
    ]
    for one in loads:
        one.start()

    peers = x_dev[1:] + y_dev[1:] + z_dev[1:] + [p_dev, k_dev]
    barrier = pltpu.get_barrier_semaphore()
    for peer in peers:
        pl.semaphore_signal(barrier, inc=1, device_id=peer, device_id_type=MESH)
    q_me = p * NZ + z
    for f in range(NS):
        loads[f].wait()
        gat[f, k, q_me] = fold(first[f].astype(F32)).astype(BF16)
    pl.semaphore_wait(barrier, len(peers))

    def gat_at(f, k_, p_, d):
        return gat.at[f, k_, p_ * NZ + add(z, -d, NZ)]

    def forward(f, d):
        blk = gat_at(f, k, p, d)
        if d:
            copy(blk, blk, az_s.at[f, d], az_r.at[f, d], z_dev[d]).wait_recv()
        start(blk, blk, ay_s.at[f, d], ay_r.at[f, d], p_dev)
        start(blk, blk, ak_s.at[f, 0, d], ak_r.at[f, 0, d], k_dev)

    def forward_pair(f, d):
        blk = gat_at(f, k, np_, d)
        copy(blk, blk, ay_s.at[f, d], ay_r.at[f, d], p_dev).wait_recv()
        start(blk, blk, ak_s.at[f, 1, d], ak_r.at[f, 1, d], k_dev)

    def row_terms(f, d0):
        for d in (d0, d0 + 4):
            for side, p_ in ((0, p), (1, np_)):
                blk = gat_at(f, nk, p_, d)
                copy(blk, blk, ak_s.at[f, side, d], ak_r.at[f, side, d], k_dev).wait_recv()
        xt = add(z, -d0, NX)
        for j in range(NY):
            q = j * NX + xt
            both = [unfold(gat[f, i, q].astype(F32)) for i in range(NK)]
            rows[f, xt, pl.ds(16 * j, 16), :] = jnp.concatenate(both, 0).astype(BF16)
        term = dot(rows[f, xt], weights[f], ((1,), (f,)))
        dx = add(xt, -x, NX)

        @pl.when(dx == 0)
        def _():
            own[f] = term.reshape(NY, 16, WIDTH)

        @pl.when(dx != 0)
        def _():
            xs[f, xt] = term.astype(BF16).reshape(NY, 16, WIDTH)
            copy(
                xs.at[f, xt], xr.at[f, dx], rx_s.at[f, dx], rx_r.at[f, dx], row_dev(yh, xt)
            ).start()

    for f in range(NS):
        mine = gat.at[f, k, q_me]
        for d in Z_ORDER:
            start(mine, mine, az_s.at[f, d], az_r.at[f, d], z_dev[d])
        forward(f, 0)
    for d in Z_ORDER:
        forward(0, d)
    forward_pair(0, 0)
    for d in Z_ORDER:
        forward_pair(0, d)
        forward(1, d)
    loads[2].wait()
    row_terms(0, 0)
    forward_pair(1, 0)
    forward_pair(1, 4)
    row_terms(0, 3)
    forward_pair(1, 3)
    forward_pair(1, 5)
    row_terms(0, 1)
    forward_pair(1, 1)
    forward_pair(1, 7)
    row_terms(0, 2)
    forward_pair(1, 2)
    forward_pair(1, 6)
    loads[3].wait()
    for d in (0, 3, 1, 2):
        row_terms(1, d)

    def x_sums(f):
        for d in range(1, NX):
            one = copy(xs.at[f, 0], xr.at[f, d], rx_s.at[f, d], rx_r.at[f, d], x_dev[d])
            one.wait_recv()
            one.wait_send()

        def total(j):
            return own[f, j] + sum(xr[f, d, j].astype(F32) for d in range(1, NX))

        for d in (2, 1, 3):
            ys[f, d] = total(add(yh, d, NY)).astype(BF16)
            start(ys.at[f, d], yr.at[f, d], ry_s.at[f, d], ry_r.at[f, d], y_dev[d])
        own[f, yh] = total(yh)

    def y_sums(f):
        total = own[f, yh]
        for d in (1, 3, 2):
            copy(ys.at[f, d], yr.at[f, d], ry_s.at[f, d], ry_r.at[f, d], y_dev[d]).wait_recv()
            total = total + yr[f, d].astype(F32)
        return total

    def spread(f):
        mine = act.at[f, x, yh]
        for d in (2, 1, 3):
            start(mine, mine, cy_s.at[f, d], cy_r.at[f, d], y_dev[d])
        for e in (2, 1, 3):
            start(mine, mine, cx_s.at[f, 0, e], cx_r.at[f, 0, e], x_dev[e])

    def spread_on(f):
        for d in (1, 3, 2):
            blk = act.at[f, x, add(yh, -d, NY)]
            copy(blk, blk, cy_s.at[f, d], cy_r.at[f, d], y_dev[d]).wait_recv()
            for e in (2, 1, 3):
                start(blk, blk, cx_s.at[f, d, e], cx_r.at[f, d, e], x_dev[e])

    x_sums(0)
    value, slope = gelu_parts(y_sums(0))
    act[0, x, yh] = value.astype(BF16)
    spread(0)
    slopes[...] = slope
    x_sums(1)
    spread_on(0)
    act[1, x, yh] = (y_sums(1) * slopes[...]).astype(BF16)
    spread(1)

    def unit_terms(f, e):
        xt = add(x, -e, NX)
        if e:
            for d in (0, 1, 3, 2):
                blk = act.at[f, xt, add(yh, -d, NY)]
                copy(blk, blk, cx_s.at[f, d, e], cx_r.at[f, d, e], x_dev[e]).wait_recv()
        term = dot(act[f, xt].reshape(64, WIDTH), weights[1 - f], ((1,), (f,)))
        for j in range(NY):
            two = [fold(term[16 * j + 8 * i:16 * j + 8 * i + 8]) for i in range(NK)]
            part[f, e, j] = jnp.where(k == 0, two[0], two[1])
            ss[f, e, j] = jnp.where(k == 0, two[1], two[0])
        start(ss.at[f, e], sr.at[f, e], dk_s.at[f, e], dk_r.at[f, e], k_dev)

    def core_sums(f, e):
        copy(ss.at[f, e], sr.at[f, e], dk_s.at[f, e], dk_r.at[f, e], k_dev).wait_recv()
        for i in range(2):
            j = 2 * np_ + i
            ps[f, e, i] = (part[f, e, j] + sr[f, e, j]).astype(BF16)
        start(ps.at[f, e], pr.at[f, e], dy_s.at[f, e], dy_r.at[f, e], p_dev)

    def pair_sums(f, e):
        copy(ps.at[f, e], pr.at[f, e], dy_s.at[f, e], dy_r.at[f, e], p_dev).wait_recv()
        for i in range(2):
            j = 2 * p + i
            zt = NX * i + add(x, -e, NX)
            total = part[f, e, j] + sr[f, e, j] + pr[f, e, i].astype(F32)
            dz = add(zt, -z, NZ)

            @pl.when(dz == 0)
            def _():
                part[f, 0, 2 * np_] = total

            @pl.when(dz != 0)
            def _():
                zs[f, dz] = total.astype(BF16)
                copy(
                    zs.at[f, dz], zr.at[f, dz], dz_s.at[f, dz], dz_r.at[f, dz], col_dev(p, zt, k)
                ).start()

    def z_sums(f, out):
        total = part[f, 0, 2 * np_]
        for d in range(1, NZ):
            one = copy(zs.at[f, d], zr.at[f, d], dz_s.at[f, d], dz_r.at[f, d], z_dev[d])
            one.wait_recv()
            one.wait_send()
            total = total + zr[f, d].astype(F32)
        out[...] = unfold(total).astype(BF16)

    def grad(left, right, out):
        for m in range(3):
            cols = slice(256 * m, 256 * m + 256)
            out[:, cols] = dot(left, right[:, cols], ((0,), (0,))).astype(BF16)

    order = (0, 1, 3, 2)
    for e in order:
        unit_terms(0, e)
    spread_on(1)
    for e in order:
        core_sums(0, e)
    grad(act[0].reshape(256, WIDTH), rows[1].reshape(256, WIDTH), go)
    for e in order:
        unit_terms(1, e)
    for e in order:
        pair_sums(0, e)
    for e in order:
        core_sums(1, e)
    grad(rows[0].reshape(256, WIDTH), act[1].reshape(256, WIDTH), gi)
    for e in order:
        pair_sums(1, e)
    z_sums(0, mixed_ref)
    z_sums(1, gt_ref)

    for one in sends:
        one.wait_send()


def write_out(*refs):
    sems = refs[-1]
    copies = [pltpu.make_async_copy(refs[i], refs[4 + i], sems.at[i]) for i in range(4)]
    for one in copies:
        one.start()
    for one in copies:
        one.wait()


def shards(tokens, cotangent, weight_in, weight_out):
    dma = pltpu.SemaphoreType.DMA
    vmem, anywhere = pl.BlockSpec(memory_space=pltpu.VMEM), pl.BlockSpec(memory_space=pl.ANY)
    shape = lambda a: jax.ShapeDtypeStruct(a.shape, BF16)
    sem = lambda *n: [dma(n), dma(n)]
    outs = pl.pallas_call(
        kernel,
        out_shape=(shape(tokens), shape(tokens), shape(weight_in), shape(weight_out)),
        in_specs=[anywhere] * 4,
        out_specs=(vmem,) * 4,
        scratch_shapes=[
            pltpu.VMEM((NS, WIDTH, WIDTH), BF16),
            pltpu.VMEM((NS, 8, WIDTH), BF16),
            pltpu.VMEM((NS, NK, NP * NZ, 16, HALF), BF16),
            pltpu.VMEM((NS, NX, 64, WIDTH), BF16),
            pltpu.VMEM((NS, NY, 16, WIDTH), F32),
            pltpu.VMEM((NS, NX, NY, 16, WIDTH), BF16),
            pltpu.VMEM((NS, NX, NY, 16, WIDTH), BF16),
            pltpu.VMEM((NS, NY, 16, WIDTH), BF16),
            pltpu.VMEM((NS, NY, 16, WIDTH), BF16),
            pltpu.VMEM((16, WIDTH), F32),
            pltpu.VMEM((NS, NX, NY, 16, WIDTH), BF16),
            pltpu.VMEM((NS, NX, NY, 16, HALF), F32),
            pltpu.VMEM((NS, NX, NY, 16, HALF), F32),
            pltpu.VMEM((NS, NX, NY, 16, HALF), F32),
            pltpu.VMEM((NS, NX, 2, 16, HALF), BF16),
            pltpu.VMEM((NS, NX, 2, 16, HALF), BF16),
            pltpu.VMEM((NS, NZ, 16, HALF), BF16),
            pltpu.VMEM((NS, NZ, 16, HALF), BF16),
            dma((4,)),
            *sem(NS, NZ), *sem(NS, NZ), *sem(NS, 2, NZ),
            *sem(NS, NX), *sem(NS, NY),
            *sem(NS, NY), *sem(NS, NY, NX),
            *sem(NS, NX), *sem(NS, NX), *sem(NS, NZ),
        ],
        compiler_params=pltpu.CompilerParams(
            collective_id=0, has_side_effects=True, vmem_limit_bytes=51 * 2**20
        ),
    )(tokens, cotangent, weight_in, weight_out)
    return pl.pallas_call(
        write_out,
        out_shape=tuple(shape(a) for a in outs),
        in_specs=[anywhere] * 4,
        out_specs=(anywhere,) * 4,
        scratch_shapes=[dma((4,))],
        compiler_params=pltpu.CompilerParams(vmem_limit_bytes=2**20),
    )(*outs)


def solution(mesh):
    return jax.shard_map(
        shards,
        mesh=mesh,
        in_specs=(P("col", "row"), P("col", "row"), P("row", "col"), P("col", "row")),
        out_specs=(P("col", "row"), P("col", "row"), P("row", "col"), P("col", "row")),
        check_vma=False,
    )
```

time: 521 us -> 69.2 us (0.13)
  the two profiles are of different devices: /device:TPU:4 before, /device:TPU:8 now
where the time goes in v2:
time: 69.2 us; the launch traced here: 69 us
  Pallas kernels  66.9 us (97%)
  local copies, waits for them, and re-layouts  1.41 us (2%)
    pallas_call x1, Pallas kernels, shards(): pl.pallas_call(kernel, out_shape=(shape(tokens), shape(tokens), shape(wei...  65.5 us
    pallas_call x1, Pallas kernels, shards(): pl.pallas_call(write_out, out_shape=tuple((shape(a) for a in outs)), in_s...  1.45 us
    unnamed x4, local copies, waits for them, and re-layouts  1.41 us

profile of v2, /device:TPU:8, one launch (start us, length us, event | category | flops | bytes accessed | tf_op | source)
XLA Modules:
  0.0 69.0 jit_solution(4076149919042211300)
XLA Ops:
  0.6 0.0 copy-start
  0.6 0.7 %copy-done = bf16[8,768]{1,0:T(8,128)(2,1)S(1)} copy-done((bf16[8,768]{1,0:T(8,128)(2,1)S(1)}, bf16[8,768]{1,0:T(8,128)(2,1)}, u32[]{:S(2)}) %copy-start) | copy-done | bytes 12312
  1.3 0.0 copy-start.1
  1.3 0.7 %copy-done.1 = bf16[8,768]{1,0:T(8,128)(2,1)S(1)} copy-done((bf16[8,768]{1,0:T(8,128)(2,1)S(1)}, bf16[8,768]{1,0:T(8,128)(2,1)}, u32[]{:S(2)}) %copy-start.1) | copy-done | bytes 12312
  2.0 65.5 %shard_map.75 = (bf16[8,768]{1,0:T(8,128)(2,1)S(1)}, bf16[8,768]{1,0:T(8,128)(2,1)S(1)}, bf16[768,768]{1,0:T(8,128)(2,1)S(1)}, bf16[768,768]{1,0:T(8,128)(2,1)S(1)}) custom-call(bf16[8,768]{1,0:T(8,128)(2,1)S(1)} %copy-done, bf16[8,768]{1,0:T(8,128)(2,1)S(1)} %copy-done.1, bf16[768,768]{1,0:T(8,128)(2,1)} %wi_hbm.1, bf16[768,768]{1,0:T(8,128)(2,1)} %wo_hbm.1), custom_call_target="tpu_custom_call" | custom-call | tf_op jit(solution)/shard_map/pallas_call | solution.py:298
  67.5 1.4 %shard_map.76 = (bf16[8,768]{1,0:T(8,128)(2,1)}, bf16[8,768]{1,0:T(8,128)(2,1)}, bf16[768,768]{1,0:T(8,128)(2,1)}, bf16[768,768]{1,0:T(8,128)(2,1)}) custom-call(bf16[8,768]{1,0:T(8,128)(2,1)S(1)} %get-tuple-element.8.refs_0_, bf16[8,768]{1,0:T(8,128)(2,1)S(1)} %get-tuple-element.9.refs_1_, bf16[768,768]{1,0:T(8,128)(2,1)S(1)} %get-tuple-element.10.refs_2_, ...), custom_call_target="tpu_custom_call" | custom-call | tf_op jit(solution)/shard_map/pallas_call | solution.py:332
Async XLA Ops:
  0.6 0.7 %copy-start = (bf16[8,768]{1,0:T(8,128)(2,1)S(1)}, bf16[8,768]{1,0:T(8,128)(2,1)}, u32[]{:S(2)}) copy-start(bf16[8,768]{1,0:T(8,128)(2,1)} %tok_hbm.1) | copy-start | bytes 36868
  1.3 0.7 %copy-start.1 = (bf16[8,768]{1,0:T(8,128)(2,1)S(1)}, bf16[8,768]{1,0:T(8,128)(2,1)}, u32[]{:S(2)}) copy-start(bf16[8,768]{1,0:T(8,128)(2,1)} %cot_hbm.1) | copy-start | bytes 36868

commit v3 on v2

--- a/solution.py
+++ b/solution.py
@@ -10,7 +10,8 @@
 NX, NY, NP, NZ, NK = 4, 4, 2, 8, 2
 NS = 2
 WIDTH, HALF = 768, 384
-Z_ORDER = (4, 3, 5, 1, 7, 2, 6)
+Z_ORDER = (0, 4, 3, 7, 5, 1, 2, 6)
+SLOT = {d: i for i, d in enumerate(Z_ORDER)}
 
 
 def gelu_parts(pre_act):
@@ -87,38 +88,48 @@
     barrier = pltpu.get_barrier_semaphore()
     for peer in peers:
         pl.semaphore_signal(barrier, inc=1, device_id=peer, device_id_type=MESH)
-    q_me = p * NZ + z
     for f in range(NS):
         loads[f].wait()
-        gat[f, k, q_me] = fold(first[f].astype(F32)).astype(BF16)
+        gat[f, k, p, 0] = fold(first[f].astype(F32)).astype(BF16)
     pl.semaphore_wait(barrier, len(peers))
 
-    def gat_at(f, k_, p_, d):
-        return gat.at[f, k_, p_ * NZ + add(z, -d, NZ)]
-
-    def forward(f, d):
-        blk = gat_at(f, k, p, d)
-        if d:
-            copy(blk, blk, az_s.at[f, d], az_r.at[f, d], z_dev[d]).wait_recv()
-        start(blk, blk, ay_s.at[f, d], ay_r.at[f, d], p_dev)
-        start(blk, blk, ak_s.at[f, 0, d], ak_r.at[f, 0, d], k_dev)
-
-    def forward_pair(f, d):
-        blk = gat_at(f, k, np_, d)
-        copy(blk, blk, ay_s.at[f, d], ay_r.at[f, d], p_dev).wait_recv()
-        start(blk, blk, ak_s.at[f, 1, d], ak_r.at[f, 1, d], k_dev)
+    for f in range(NS):
+        for d in Z_ORDER[1:]:
+            start(
+                gat.at[f, k, p, 0], gat.at[f, k, p, SLOT[d]],
+                az_s.at[f, d], az_r.at[f, d], z_dev[d],
+            )
+
+    def half(f, k_, p_, h):
+        return gat.at[f, k_, p_, pl.ds(4 * h, 4)]
+
+    def forward(f, h):
+        for d in Z_ORDER[4 * h:4 * h + 4]:
+            if d:
+                blk = gat.at[f, k, p, SLOT[d]]
+                copy(blk, blk, az_s.at[f, d], az_r.at[f, d], z_dev[d]).wait_recv()
+        blk = half(f, k, p, h)
+        start(blk, blk, ay_s.at[f, h], ay_r.at[f, h], p_dev)
+        start(blk, blk, ak_s.at[f, 0, h], ak_r.at[f, 0, h], k_dev)
+
+    def forward_pair(f, h):
+        blk = half(f, k, np_, h)
+        copy(blk, blk, ay_s.at[f, h], ay_r.at[f, h], p_dev).wait_recv()
+        start(blk, blk, ak_s.at[f, 1, h], ak_r.at[f, 1, h], k_dev)
+
+    def core_arrived(f, h):
+        for side, p_ in ((0, p), (1, np_)):
+            blk = half(f, nk, p_, h)
+            copy(blk, blk, ak_s.at[f, side, h], ak_r.at[f, side, h], k_dev).wait_recv()
 
     def row_terms(f, d0):
+        xt = lax.rem(z - d0 + NZ, NX)
         for d in (d0, d0 + 4):
-            for side, p_ in ((0, p), (1, np_)):
-                blk = gat_at(f, nk, p_, d)
-                copy(blk, blk, ak_s.at[f, side, d], ak_r.at[f, side, d], k_dev).wait_recv()
-        xt = add(z, -d0, NX)
-        for j in range(NY):
-            q = j * NX + xt
-            both = [unfold(gat[f, i, q].astype(F32)) for i in range(NK)]
-            rows[f, xt, pl.ds(16 * j, 16), :] = jnp.concatenate(both, 0).astype(BF16)
-        term = dot(rows[f, xt], weights[f], ((1,), (f,)))
+            high = add(z, -d, NZ) // NX
+            for p_ in range(NP):
+                both = [unfold(gat[f, i, p_, SLOT[d]].astype(F32)) for i in range(NK)]
+                rows[f, xt, 2 * p_ + high] = jnp.concatenate(both, 0).astype(BF16)
+        term = dot(rows[f, xt].reshape(64, WIDTH), weights[f], ((1,), (f,)))
         dx = add(xt, -x, NX)
 
         @pl.when(dx == 0)
@@ -132,33 +143,28 @@
                 xs.at[f, xt], xr.at[f, dx], rx_s.at[f, dx], rx_r.at[f, dx], row_dev(yh, xt)
             ).start()
 
-    for f in range(NS):
-        mine = gat.at[f, k, q_me]
-        for d in Z_ORDER:
-            start(mine, mine, az_s.at[f, d], az_r.at[f, d], z_dev[d])
-        forward(f, 0)
-    for d in Z_ORDER:
-        forward(0, d)
+    forward(0, 0)
+    forward(0, 1)
     forward_pair(0, 0)
-    for d in Z_ORDER:
-        forward_pair(0, d)
-        forward(1, d)
+    forward(1, 0)
     loads[2].wait()
+    core_arrived(0, 0)
     row_terms(0, 0)
+    forward_pair(0, 1)
+    row_terms(0, 3)
+    forward(1, 1)
+    core_arrived(0, 1)
+    row_terms(0, 1)
+    row_terms(0, 2)
     forward_pair(1, 0)
-    forward_pair(1, 4)
-    row_terms(0, 3)
-    forward_pair(1, 3)
-    forward_pair(1, 5)
-    row_terms(0, 1)
     forward_pair(1, 1)
-    forward_pair(1, 7)
-    row_terms(0, 2)
-    forward_pair(1, 2)
-    forward_pair(1, 6)
     loads[3].wait()
-    for d in (0, 3, 1, 2):
-        row_terms(1, d)
+    core_arrived(1, 0)
+    row_terms(1, 0)
+    row_terms(1, 3)
+    core_arrived(1, 1)
+    row_terms(1, 1)
+    row_terms(1, 2)
 
     def x_sums(f):
         for d in range(1, NX):
@@ -186,14 +192,14 @@
         for d in (2, 1, 3):
             start(mine, mine, cy_s.at[f, d], cy_r.at[f, d], y_dev[d])
         for e in (2, 1, 3):
-            start(mine, mine, cx_s.at[f, 0, e], cx_r.at[f, 0, e], x_dev[e])
+            start(mine, mine, cx_s.at[f, 0, e], cx_r.at[f, e], x_dev[e])
 
     def spread_on(f):
         for d in (1, 3, 2):
             blk = act.at[f, x, add(yh, -d, NY)]
             copy(blk, blk, cy_s.at[f, d], cy_r.at[f, d], y_dev[d]).wait_recv()
             for e in (2, 1, 3):
-                start(blk, blk, cx_s.at[f, d, e], cx_r.at[f, d, e], x_dev[e])
+                start(blk, blk, cx_s.at[f, d, e], cx_r.at[f, e], x_dev[e])
 
     x_sums(0)
     value, slope = gelu_parts(y_sums(0))
@@ -208,9 +214,8 @@
     def unit_terms(f, e):
         xt = add(x, -e, NX)
         if e:
-            for d in (0, 1, 3, 2):
-                blk = act.at[f, xt, add(yh, -d, NY)]
-                copy(blk, blk, cx_s.at[f, d, e], cx_r.at[f, d, e], x_dev[e]).wait_recv()
+            blk = act.at[f, xt]
+            copy(blk, blk, cx_s.at[f, 0, e], cx_r.at[f, e], x_dev[e]).wait_recv()
         term = dot(act[f, xt].reshape(64, WIDTH), weights[1 - f], ((1,), (f,)))
         for j in range(NY):
             two = [fold(term[16 * j + 8 * i:16 * j + 8 * i + 8]) for i in range(NK)]
@@ -258,6 +263,10 @@
             cols = slice(256 * m, 256 * m + 256)
             out[:, cols] = dot(left, right[:, cols], ((0,), (0,))).astype(BF16)
 
+    def drain():
+        for one in sends:
+            one.wait_send()
+
     order = (0, 1, 3, 2)
     for e in order:
         unit_terms(0, e)
@@ -272,13 +281,11 @@
     for e in order:
         core_sums(1, e)
     grad(rows[0].reshape(256, WIDTH), act[1].reshape(256, WIDTH), gi)
+    drain()
     for e in order:
         pair_sums(1, e)
     z_sums(0, mixed_ref)
     z_sums(1, gt_ref)
-
-    for one in sends:
-        one.wait_send()
 
 
 def write_out(*refs):
@@ -303,8 +310,8 @@
         scratch_shapes=[
             pltpu.VMEM((NS, WIDTH, WIDTH), BF16),
             pltpu.VMEM((NS, 8, WIDTH), BF16),
-            pltpu.VMEM((NS, NK, NP * NZ, 16, HALF), BF16),
-            pltpu.VMEM((NS, NX, 64, WIDTH), BF16),
+            pltpu.VMEM((NS, NK, NP, NZ, 16, HALF), BF16),
+            pltpu.VMEM((NS, NX, NY, 16, WIDTH), BF16),
             pltpu.VMEM((NS, NY, 16, WIDTH), F32),
             pltpu.VMEM((NS, NX, NY, 16, WIDTH), BF16),
             pltpu.VMEM((NS, NX, NY, 16, WIDTH), BF16),
@@ -320,9 +327,9 @@
             pltpu.VMEM((NS, NZ, 16, HALF), BF16),
             pltpu.VMEM((NS, NZ, 16, HALF), BF16),
             dma((4,)),
-            *sem(NS, NZ), *sem(NS, NZ), *sem(NS, 2, NZ),
+            *sem(NS, NZ), *sem(NS, 2), *sem(NS, 2, 2),
             *sem(NS, NX), *sem(NS, NY),
-            *sem(NS, NY), *sem(NS, NY, NX),
+            *sem(NS, NY), dma((NS, NY, NX)), dma((NS, NX)),
             *sem(NS, NX), *sem(NS, NX), *sem(NS, NZ),
         ],
         compiler_params=pltpu.CompilerParams(

time: 69.2 us -> 69.1 us (level)
  the two profiles are of different devices: /device:TPU:8 before, /device:TPU:2 now
where the time goes in v3:
time: 69.1 us; the launch traced here: 68.8 us
  Pallas kernels  66.8 us (97%)
  local copies, waits for them, and re-layouts  1.41 us (2%)
    pallas_call x1, Pallas kernels, shards(): pl.pallas_call(kernel, out_shape=(shape(tokens), shape(tokens), shape(wei...  65.3 us
    pallas_call x1, Pallas kernels, shards(): pl.pallas_call(write_out, out_shape=tuple((shape(a) for a in outs)), in_s...  1.45 us
    unnamed x4, local copies, waits for them, and re-layouts  1.41 us

profile of v3, /device:TPU:2, one launch (start us, length us, event | category | flops | bytes accessed | tf_op | source)
XLA Modules:
  0.0 68.8 jit_solution(16698461903039141347)
XLA Ops:
  0.6 0.0 copy-start
  0.6 0.7 %copy-done = bf16[8,768]{1,0:T(8,128)(2,1)S(1)} copy-done((bf16[8,768]{1,0:T(8,128)(2,1)S(1)}, bf16[8,768]{1,0:T(8,128)(2,1)}, u32[]{:S(2)}) %copy-start) | copy-done | bytes 12312
  1.3 0.0 copy-start.1
  1.3 0.7 %copy-done.1 = bf16[8,768]{1,0:T(8,128)(2,1)S(1)} copy-done((bf16[8,768]{1,0:T(8,128)(2,1)S(1)}, bf16[8,768]{1,0:T(8,128)(2,1)}, u32[]{:S(2)}) %copy-start.1) | copy-done | bytes 12312
  2.0 65.3 %shard_map.75 = (bf16[8,768]{1,0:T(8,128)(2,1)S(1)}, bf16[8,768]{1,0:T(8,128)(2,1)S(1)}, bf16[768,768]{1,0:T(8,128)(2,1)S(1)}, bf16[768,768]{1,0:T(8,128)(2,1)S(1)}) custom-call(bf16[8,768]{1,0:T(8,128)(2,1)S(1)} %copy-done, bf16[8,768]{1,0:T(8,128)(2,1)S(1)} %copy-done.1, bf16[768,768]{1,0:T(8,128)(2,1)} %wi_hbm.1, bf16[768,768]{1,0:T(8,128)(2,1)} %wo_hbm.1), custom_call_target="tpu_custom_call" | custom-call | tf_op jit(solution)/shard_map/pallas_call | solution.py:305
  67.4 1.4 %shard_map.76 = (bf16[8,768]{1,0:T(8,128)(2,1)}, bf16[8,768]{1,0:T(8,128)(2,1)}, bf16[768,768]{1,0:T(8,128)(2,1)}, bf16[768,768]{1,0:T(8,128)(2,1)}) custom-call(bf16[8,768]{1,0:T(8,128)(2,1)S(1)} %get-tuple-element.8.refs_0_, bf16[8,768]{1,0:T(8,128)(2,1)S(1)} %get-tuple-element.9.refs_1_, bf16[768,768]{1,0:T(8,128)(2,1)S(1)} %get-tuple-element.10.refs_2_, ...), custom_call_target="tpu_custom_call" | custom-call | tf_op jit(solution)/shard_map/pallas_call | solution.py:339
Async XLA Ops:
  0.6 0.7 %copy-start = (bf16[8,768]{1,0:T(8,128)(2,1)S(1)}, bf16[8,768]{1,0:T(8,128)(2,1)}, u32[]{:S(2)}) copy-start(bf16[8,768]{1,0:T(8,128)(2,1)} %tok_hbm.1) | copy-start | bytes 36868
  1.3 0.7 %copy-start.1 = (bf16[8,768]{1,0:T(8,128)(2,1)S(1)}, bf16[8,768]{1,0:T(8,128)(2,1)}, u32[]{:S(2)}) copy-start(bf16[8,768]{1,0:T(8,128)(2,1)} %cot_hbm.1) | copy-start | bytes 36868

commit v4 on v3

--- a/solution.py
+++ b/solution.py
@@ -33,9 +33,9 @@
 
 
 def kernel(
-    tok_hbm, cot_hbm, wi_hbm, wo_hbm,
+    tok_ref, cot_ref, wi_hbm, wo_hbm,
     mixed_ref, gt_ref, gi, go,
-    weights, first, gat, rows, own, xs, xr, ys, yr, slopes, act,
+    weights, gat, rows, own, xs, xr, ys, yr, slopes, act,
     part, ss, sr, ps, pr, zs, zr,
     w_sem,
     az_s, az_r, ay_s, ay_r, ak_s, ak_r,
@@ -78,7 +78,7 @@
     loads = [
         pltpu.make_async_copy(src, dst, w_sem.at[n])
         for n, (src, dst) in enumerate(
-            ((tok_hbm, first.at[0]), (cot_hbm, first.at[1]), (wi_hbm, weights.at[0]), (wo_hbm, weights.at[1]))
+            ((wi_hbm, weights.at[0]), (wo_hbm, weights.at[1]))
         )
     ]
     for one in loads:
@@ -89,8 +89,7 @@
     for peer in peers:
         pl.semaphore_signal(barrier, inc=1, device_id=peer, device_id_type=MESH)
     for f in range(NS):
-        loads[f].wait()
-        gat[f, k, p, 0] = fold(first[f].astype(F32)).astype(BF16)
+        gat[f, k, p, 0] = fold((tok_ref, cot_ref)[f][...].astype(F32)).astype(BF16)
     pl.semaphore_wait(barrier, len(peers))
 
     for f in range(NS):
@@ -147,7 +146,7 @@
     forward(0, 1)
     forward_pair(0, 0)
     forward(1, 0)
-    loads[2].wait()
+    loads[0].wait()
     core_arrived(0, 0)
     row_terms(0, 0)
     forward_pair(0, 1)
@@ -158,7 +157,7 @@
     row_terms(0, 2)
     forward_pair(1, 0)
     forward_pair(1, 1)
-    loads[3].wait()
+    loads[1].wait()
     core_arrived(1, 0)
     row_terms(1, 0)
     row_terms(1, 3)
@@ -288,11 +287,15 @@
     z_sums(1, gt_ref)
 
 
-def write_out(*refs):
-    sems = refs[-1]
-    copies = [pltpu.make_async_copy(refs[i], refs[4 + i], sems.at[i]) for i in range(4)]
+def write_out(mixed, gt, gi, go, mixed_out, gt_out, gi_out, go_out, sems):
+    copies = [
+        pltpu.make_async_copy(gi, gi_out, sems.at[0]),
+        pltpu.make_async_copy(go, go_out, sems.at[1]),
+    ]
     for one in copies:
         one.start()
+    mixed_out[...] = mixed[...]
+    gt_out[...] = gt[...]
     for one in copies:
         one.wait()
 
@@ -305,11 +308,10 @@
     outs = pl.pallas_call(
         kernel,
         out_shape=(shape(tokens), shape(tokens), shape(weight_in), shape(weight_out)),
-        in_specs=[anywhere] * 4,
+        in_specs=[vmem, vmem, anywhere, anywhere],
         out_specs=(vmem,) * 4,
         scratch_shapes=[
             pltpu.VMEM((NS, WIDTH, WIDTH), BF16),
-            pltpu.VMEM((NS, 8, WIDTH), BF16),
             pltpu.VMEM((NS, NK, NP, NZ, 16, HALF), BF16),
             pltpu.VMEM((NS, NX, NY, 16, WIDTH), BF16),
             pltpu.VMEM((NS, NY, 16, WIDTH), F32),
@@ -326,7 +328,7 @@
             pltpu.VMEM((NS, NX, 2, 16, HALF), BF16),
             pltpu.VMEM((NS, NZ, 16, HALF), BF16),
             pltpu.VMEM((NS, NZ, 16, HALF), BF16),
-            dma((4,)),
+            dma((2,)),
             *sem(NS, NZ), *sem(NS, 2), *sem(NS, 2, 2),
             *sem(NS, NX), *sem(NS, NY),
             *sem(NS, NY), dma((NS, NY, NX)), dma((NS, NX)),
@@ -339,9 +341,9 @@
     return pl.pallas_call(
         write_out,
         out_shape=tuple(shape(a) for a in outs),
-        in_specs=[anywhere] * 4,
-        out_specs=(anywhere,) * 4,
-        scratch_shapes=[dma((4,))],
+        in_specs=[vmem, vmem, anywhere, anywhere],
+        out_specs=(vmem, vmem, anywhere, anywhere),
+        scratch_shapes=[dma((2,))],
         compiler_params=pltpu.CompilerParams(vmem_limit_bytes=2**20),
     )(*outs)
 

time: 69.1 us -> 69.5 us (level)
  no operation moved by 1% of the time
where the time goes in v4:
time: 69.5 us; the launch traced here: 69.3 us
  Pallas kernels  67.2 us (97%)
  local copies, waits for them, and re-layouts  1.41 us (2%)
    pallas_call x1, Pallas kernels, shards(): pl.pallas_call(kernel, out_shape=(shape(tokens), shape(tokens), shape(wei...  65.2 us
    pallas_call x1, Pallas kernels, shards(): pl.pallas_call(write_out, out_shape=tuple((shape(a) for a in outs)), in_s...  2.02 us
    unnamed x4, local copies, waits for them, and re-layouts  1.41 us

profile of v4, /device:TPU:2, one launch (start us, length us, event | category | flops | bytes accessed | tf_op | source)
XLA Modules:
  0.0 69.3 jit_solution(11869089415955573144)
XLA Ops:
  0.6 0.0 copy-start
  0.6 0.7 %copy-done = bf16[8,768]{1,0:T(8,128)(2,1)S(1)} copy-done((bf16[8,768]{1,0:T(8,128)(2,1)S(1)}, bf16[8,768]{1,0:T(8,128)(2,1)}, u32[]{:S(2)}) %copy-start) | copy-done | bytes 12312
  1.3 0.0 copy-start.1
  1.3 0.7 %copy-done.1 = bf16[8,768]{1,0:T(8,128)(2,1)S(1)} copy-done((bf16[8,768]{1,0:T(8,128)(2,1)S(1)}, bf16[8,768]{1,0:T(8,128)(2,1)}, u32[]{:S(2)}) %copy-start.1) | copy-done | bytes 12312
  2.0 65.2 %shard_map.75 = (bf16[8,768]{1,0:T(8,128)(2,1)S(1)}, bf16[8,768]{1,0:T(8,128)(2,1)S(1)}, bf16[768,768]{1,0:T(8,128)(2,1)S(1)}, bf16[768,768]{1,0:T(8,128)(2,1)S(1)}) custom-call(bf16[8,768]{1,0:T(8,128)(2,1)S(1)} %copy-done, bf16[8,768]{1,0:T(8,128)(2,1)S(1)} %copy-done.1, bf16[768,768]{1,0:T(8,128)(2,1)} %wi_hbm.1, bf16[768,768]{1,0:T(8,128)(2,1)} %wo_hbm.1), custom_call_target="tpu_custom_call" | custom-call | tf_op jit(solution)/shard_map/pallas_call | solution.py:308
  67.3 2.0 %shard_map.76 = (bf16[8,768]{1,0:T(8,128)(2,1)}, bf16[8,768]{1,0:T(8,128)(2,1)}, bf16[768,768]{1,0:T(8,128)(2,1)}, bf16[768,768]{1,0:T(8,128)(2,1)}) custom-call(bf16[8,768]{1,0:T(8,128)(2,1)S(1)} %get-tuple-element.8.mixed, bf16[8,768]{1,0:T(8,128)(2,1)S(1)} %get-tuple-element.9.gt, bf16[768,768]{1,0:T(8,128)(2,1)S(1)} %get-tuple-element.10.gi, ...), custom_call_target="tpu_custom_call" | custom-call | tf_op jit(solution)/shard_map/pallas_call | solution.py:341
Async XLA Ops:
  0.6 0.7 %copy-start = (bf16[8,768]{1,0:T(8,128)(2,1)S(1)}, bf16[8,768]{1,0:T(8,128)(2,1)}, u32[]{:S(2)}) copy-start(bf16[8,768]{1,0:T(8,128)(2,1)} %tok_ref.1) | copy-start | bytes 36868
  1.3 0.7 %copy-start.1 = (bf16[8,768]{1,0:T(8,128)(2,1)S(1)}, bf16[8,768]{1,0:T(8,128)(2,1)}, u32[]{:S(2)}) copy-start(bf16[8,768]{1,0:T(8,128)(2,1)} %cot_ref.1) | copy-start | bytes 36868
